TPU v7x, 128 devices: a whole 4x4x4 slice. The times are simulated.
128 devices in a mesh: ctx: 32 (over x_hi, y, z), fsdp: 4 (over x_lo, core).
Axes of the slice: x: 4 (x_hi: 2, x_lo: 2; x = x_hi * 2 + x_lo), y: 4, z: 4, core: 2. Of those that a mesh axis runs over, the one named last changes fastest.
Arguments:
- streams: bfloat16 [2, 4, 2048, 4, 2048], P(None, 'fsdp', 'ctx'), may hold values from -48 to 48
- doc_start: int32 [2, 4, 2048], P(None, 'fsdp', 'ctx'), may hold values from 0 to 2047, as said below
- cotangent: bfloat16 [2, 4, 2048, 4, 2048], P(None, 'fsdp', 'ctx'), may hold values from -6 to 6
- mixing: float32 [2, 4, 6], replicated, may hold values from -0.3 to 1
- w_project: float32 [2048, 2560], P(('ctx', 'fsdp')), may hold values from -0.125 to 0.125
- w_output: float32 [2048, 2048], P(('ctx', 'fsdp')), may hold values from -0.5 to 0.5
- w_expand: float32 [2048, 11264], P(('ctx', 'fsdp')), may hold values from -0.125 to 0.125
- w_reduce: float32 [5632, 2048], P(('ctx', 'fsdp')), may hold values from -0.078125 to 0.078125
- first_mixing: float32 [2, 4, 6], replicated, may hold values from -0.01953125 to 0.01953125
- second_mixing: float32 [2, 4, 6], replicated, may hold values from 7.338825e-06 to 2.9369252e-05
- first_project: float32 [2048, 2560], P(('ctx', 'fsdp')), may hold values from -0.00012207031 to 0.00012207031
- second_project: float32 [2048, 2560], P(('ctx', 'fsdp')), may hold values from 3.2250697e-10 to 1.2906409e-09
- first_output: float32 [2048, 2048], P(('ctx', 'fsdp')), may hold values from -6.1035156e-05 to 6.1035156e-05
- second_output: float32 [2048, 2048], P(('ctx', 'fsdp')), may hold values from 8.062674e-11 to 3.2266023e-10
- first_expand: float32 [2048, 11264], P(('ctx', 'fsdp')), may hold values from -0.00018310547 to 0.00018310547
- second_expand: float32 [2048, 11264], P(('ctx', 'fsdp')), may hold values from 7.2564066e-10 to 2.9039422e-09
- first_reduce: float32 [5632, 2048], P(('ctx', 'fsdp')), may hold values from -0.00036621094 to 0.00036621094
- second_reduce: float32 [5632, 2048], P(('ctx', 'fsdp')), may hold values from 2.9025626e-09 to 1.1615769e-08
Outputs:
- new_streams: bfloat16 [2, 4, 2048, 4, 2048], P(None, 'fsdp', 'ctx')
- streams_grad: float32 [2, 4, 2048, 4, 2048], P(None, 'fsdp', 'ctx')
- grad_norm: float32 [], replicated
- updated_mixing: float32 [2, 4, 6], replicated
- moment_mixing: float32 [2, 4, 6], replicated
- square_mixing: float32 [2, 4, 6], replicated
- updated_project: float32 [2048, 2560], P(('ctx', 'fsdp'))
- moment_project: float32 [2048, 2560], P(('ctx', 'fsdp'))
- square_project: float32 [2048, 2560], P(('ctx', 'fsdp'))
- updated_output: float32 [2048, 2048], P(('ctx', 'fsdp'))
- moment_output: float32 [2048, 2048], P(('ctx', 'fsdp'))
- square_output: float32 [2048, 2048], P(('ctx', 'fsdp'))
- updated_expand: float32 [2048, 11264], P(('ctx', 'fsdp'))
- moment_expand: float32 [2048, 11264], P(('ctx', 'fsdp'))
- square_expand: float32 [2048, 11264], P(('ctx', 'fsdp'))
- updated_reduce: float32 [5632, 2048], P(('ctx', 'fsdp'))
- moment_reduce: float32 [5632, 2048], P(('ctx', 'fsdp'))
- square_reduce: float32 [5632, 2048], P(('ctx', 'fsdp'))
Inputs may be any that keep to these rules, and one draw needn't show every extreme that they name: doc_start[m, b, i] is the first position of the document that holds position i of sequence (m, b): 0 at i = 0, never falling along i, at most i, and equal to i where a document begins; the last position of every sequence begins a document of its own.
All inputs are finite; a program needn't handle non-finite values.
Results may differ from a plain program's by a relative error of at most 0.019.
Values may be sent and summed in bfloat16 or wider, within the bound.
A program may use at most 640 MiB of HBM per device.

v0:
```python
import math

import jax
import jax.numpy as jnp
from jax import lax
from jax.sharding import PartitionSpec as P

H = 32
KV = 4
HD = 64
FF = 5632
MICRO = 2
STEP = 10


NORM_EPS = 1e-05
THETA_BASE = 10000.0
BETA_ONE = 0.9
BETA_TWO = 0.95
ADAM_EPS = 1e-08
RATE_MATRIX = 0.06
RATE_MIXING = 0.5
DECAY_MATRIX = 0.1
THRESHOLD = 1.0
HIGH = lax.Precision.HIGHEST


def rotary(values, spots, sign):
    half = values.shape[-1] // 2
    freq = jnp.exp(
        jnp.arange(half, dtype=jnp.float32) * (-2.0 * math.log(THETA_BASE) / values.shape[-1])
    )
    angle = spots[:, None] * freq[None, :]
    cosine = jnp.cos(angle)[:, None, :]
    sine = sign * jnp.sin(angle)[:, None, :]
    first = values[..., :half]
    second = values[..., half:]
    return jnp.concatenate(
        [first * cosine - second * sine, second * cosine + first * sine], axis=-1
    )


def mix_in(tokens, weights):
    return jnp.einsum("lsd,s->ld", tokens, weights[:, 0], precision=HIGH)


def write_back(tokens, weights, branch):
    kept = jnp.einsum("lsd,st->ltd", tokens, weights[:, 2:], precision=HIGH)
    return kept + weights[None, :, 1, None] * branch[:, None, :]


def norm_stats(entry):
    center = entry - jnp.mean(entry, axis=-1, keepdims=True)
    inverse = lax.rsqrt(jnp.mean(center * center, axis=-1, keepdims=True) + NORM_EPS)
    return (center * inverse, inverse)


def norm_back(grad, normed, inverse):
    return inverse * (
        grad
        - jnp.mean(grad, axis=-1, keepdims=True)
        - normed * jnp.mean(grad * normed, axis=-1, keepdims=True)
    )


def contract_last(left, right):
    return lax.dot_general(
        left, right, (((1,), (1,)), ((), ())), preferred_element_type=jnp.float32
    )


def contract_first(left, right):
    return lax.dot_general(
        left, right, (((0,), (0,)), ((), ())), preferred_element_type=jnp.float32
    )


def make_rows(lefts, rights):
    return jnp.concatenate(
        [contract_first(left, right) for left, right in zip(lefts, rights)], axis=1
    )


def make_down(left, right):
    return contract_first(left, right)


def scores_of(query, keys, places, starts, scale):
    pieces = keys.reshape(keys.shape[0], KV, HD)
    inner = jnp.einsum("bkgd,nkd->kgbn", query, pieces, preferred_element_type=jnp.float32) * scale
    where_keys = jnp.arange(keys.shape[0], dtype=jnp.int32)
    allowed = (where_keys[None, :] >= starts[:, None]) & (where_keys[None, :] <= places[:, None])
    return (jnp.where(allowed, inner, -1e30), allowed)


def probs_of(scored, allowed, top, total):
    return jnp.where(allowed, jnp.exp(scored - top[..., None]), 0.0) / total[..., None]


def adam(weight, grad, first, second, factor, rate, decay):
    grad = grad * factor
    first = BETA_ONE * first + (1.0 - BETA_ONE) * grad
    second = BETA_TWO * second + (1.0 - BETA_TWO) * grad * grad
    ahead = first / (1.0 - BETA_ONE**STEP)
    scaled = second / (1.0 - BETA_TWO**STEP)
    weight = weight - rate * (ahead / (jnp.sqrt(scaled) + ADAM_EPS) + decay * weight)
    return (weight, first, second)


def body(
    streams,
    doc_start,
    cotangent,
    mixing,
    w_project,
    w_output,
    w_expand,
    w_reduce,
    first_mixing,
    second_mixing,
    first_project,
    second_project,
    first_output,
    second_output,
    first_expand,
    second_expand,
    first_reduce,
    second_reduce,
):
    span = streams.shape[2]
    lanes = lax.axis_size("ctx")
    length = span * lanes
    groups = H // KV
    scale = HD ** (-0.5)
    anchor = lax.axis_index("ctx") * span
    places = anchor + jnp.arange(span, dtype=jnp.int32)
    shard_project = w_project.astype(jnp.bfloat16)
    shard_output = w_output.astype(jnp.bfloat16)
    shard_expand = w_expand.astype(jnp.bfloat16)
    shard_reduce = w_reduce.astype(jnp.bfloat16)
    outputs_new = []
    outputs_grad = []
    kept = []
    rows_grad = None
    reduce_grad = None
    mix_grad = jnp.zeros_like(mixing)
    for micro in range(MICRO):
        tokens = streams[micro, 0].astype(jnp.float32)
        starts = doc_start[micro, 0]
        spots = (places - starts).astype(jnp.float32)
        full = (
            lax.all_gather(shard_project, ("ctx", "fsdp"), axis=0, tiled=True),
            lax.all_gather(shard_output, ("ctx", "fsdp"), axis=0, tiled=True),
            lax.all_gather(shard_expand, ("ctx", "fsdp"), axis=0, tiled=True),
            lax.all_gather(shard_reduce, ("ctx", "fsdp"), axis=0, tiled=True),
        )
        full_project, full_output, full_expand, full_reduce = full
        normed_one, inverse_one = norm_stats(mix_in(tokens, mixing[0]))
        entry_one = normed_one.astype(jnp.bfloat16)
        joined = jnp.dot(entry_one, full_project, preferred_element_type=jnp.float32)
        query = (
            rotary(joined[:, : H * HD].reshape(span, H, HD), spots, 1.0)
            .astype(jnp.bfloat16)
            .reshape(span, KV, groups, HD)
        )
        keys = (
            rotary(joined[:, H * HD : (H + KV) * HD].reshape(span, KV, HD), spots, 1.0)
            .astype(jnp.bfloat16)
            .reshape(span, KV * HD)
        )
        values = joined[:, (H + KV) * HD :].astype(jnp.bfloat16)
        top_now = jnp.full((KV, groups, span), -1e30, jnp.float32)
        scored_piece, allowed_piece = scores_of(
            query, lax.all_gather(keys, "ctx", axis=0, tiled=True), places, starts, scale
        )
        fold_fresh = jnp.maximum(top_now, jnp.max(scored_piece, axis=-1))
        added = jnp.sum(
            jnp.where(allowed_piece, jnp.exp(scored_piece - fold_fresh[..., None]), 0.0), axis=-1
        )
        pieces = (
            lax.all_gather(keys, "ctx", axis=0, tiled=True),
            lax.all_gather(values, "ctx", axis=0, tiled=True),
        )
        fold_scored_piece, fold_allowed_piece = scores_of(query, pieces[0], places, starts, scale)
        weights_piece = probs_of(fold_scored_piece, fold_allowed_piece, fold_fresh, added).astype(
            jnp.bfloat16
        )
        rows = pieces[1].reshape(pieces[1].shape[0], KV, HD)
        mixed = jnp.einsum(
            "kgbn,nkd->bkgd", weights_piece, rows, preferred_element_type=jnp.float32
        )
        attended = mixed.reshape(span, H * HD).astype(jnp.bfloat16)
        branch_one = jnp.dot(attended, full_output, preferred_element_type=jnp.float32)
        middle = write_back(tokens, mixing[0], branch_one)
        normed_two, inverse_two = norm_stats(mix_in(middle, mixing[1]))
        entry_two = normed_two.astype(jnp.bfloat16)
        opened = jnp.dot(entry_two, full_expand, preferred_element_type=jnp.float32)
        gate = opened[:, :FF]
        upper = opened[:, FF:]
        hidden = (jax.nn.silu(gate) * upper).astype(jnp.bfloat16)
        branch_two = jnp.dot(hidden, full_reduce, preferred_element_type=jnp.float32)
        final = write_back(middle, mixing[1], branch_two)
        outputs_new.append(final.astype(jnp.bfloat16))
        held = lax.optimization_barrier(
            ((shard_project, shard_output, shard_expand, shard_reduce), final)
        )[0]
        back_project, back_output, back_expand, back_reduce = (
            lax.all_gather(held[0], ("ctx", "fsdp"), axis=0, tiled=True),
            lax.all_gather(held[1], ("ctx", "fsdp"), axis=0, tiled=True),
            lax.all_gather(held[2], ("ctx", "fsdp"), axis=0, tiled=True),
            lax.all_gather(held[3], ("ctx", "fsdp"), axis=0, tiled=True),
        )
        coming = cotangent[micro, 0].astype(jnp.float32)
        grad_two = jnp.einsum("ltd,t->ld", coming, mixing[1, :, 1], precision=HIGH).astype(
            jnp.bfloat16
        )
        gain_two = jnp.einsum("ld,ltd->t", branch_two, coming, precision=HIGH)
        route_two = jnp.einsum("lsd,ltd->st", middle, coming, precision=HIGH)
        back_hidden = contract_last(grad_two, back_reduce)
        sigma = jax.nn.sigmoid(gate)
        opened_grad = jnp.concatenate(
            [
                back_hidden * upper * sigma * (1.0 + gate * (1.0 - sigma)),
                back_hidden * gate * sigma,
            ],
            axis=1,
        ).astype(jnp.bfloat16)
        entry_grad_two = norm_back(contract_last(opened_grad, back_expand), normed_two, inverse_two)
        feed_two = jnp.einsum("lsd,ld->s", middle, entry_grad_two, precision=HIGH)
        middle_grad = (
            jnp.einsum("st,ltd->lsd", mixing[1, :, 2:], coming, precision=HIGH)
            + mixing[1, None, :, 0, None] * entry_grad_two[:, None, :]
        )
        grad_one = jnp.einsum("ltd,t->ld", middle_grad, mixing[0, :, 1], precision=HIGH).astype(
            jnp.bfloat16
        )
        gain_one = jnp.einsum("ld,ltd->t", branch_one, middle_grad, precision=HIGH)
        route_one = jnp.einsum("lsd,ltd->st", tokens, middle_grad, precision=HIGH)
        attended_grad = (
            contract_last(grad_one, back_output).astype(jnp.bfloat16).reshape(span, KV, groups, HD)
        )
        key_back, value_back = (
            lax.all_gather(keys, "ctx", axis=0, tiled=True),
            lax.all_gather(values, "ctx", axis=0, tiled=True),
        )
        scored, allowed = scores_of(query, key_back, places, starts, scale)
        probs = probs_of(scored, allowed, fold_fresh, added)
        keys_whole = key_back.reshape(length, KV, HD)
        values_whole = value_back.reshape(length, KV, HD)
        prob_grad = jnp.einsum(
            "bkgd,nkd->kgbn", attended_grad, values_whole, preferred_element_type=jnp.float32
        )
        score_grad = (
            probs * (prob_grad - jnp.sum(probs * prob_grad, axis=-1, keepdims=True))
        ).astype(jnp.bfloat16)
        query_grad = (
            jnp.einsum("kgbn,nkd->bkgd", score_grad, keys_whole, preferred_element_type=jnp.float32)
            * scale
        )
        key_term = (
            jnp.einsum("kgbn,bkgd->nkd", score_grad, query, preferred_element_type=jnp.float32)
            * scale
        )
        value_term = jnp.einsum(
            "kgbn,bkgd->nkd",
            probs.astype(jnp.bfloat16),
            attended_grad,
            preferred_element_type=jnp.float32,
        )
        key_grad, value_grad = (
            lax.psum_scatter(
                key_term.reshape(length, KV * HD).astype(jnp.bfloat16),
                "ctx",
                scatter_dimension=0,
                tiled=True,
            ).astype(jnp.float32),
            lax.psum_scatter(
                value_term.reshape(length, KV * HD).astype(jnp.bfloat16),
                "ctx",
                scatter_dimension=0,
                tiled=True,
            ).astype(jnp.float32),
        )
        joined_grad = jnp.concatenate(
            [
                rotary(query_grad.reshape(span, H, HD), spots, -1.0).reshape(span, H * HD),
                rotary(key_grad.reshape(span, KV, HD), spots, -1.0).reshape(span, KV * HD),
                value_grad,
            ],
            axis=1,
        ).astype(jnp.bfloat16)
        entry_grad_one = norm_back(
            contract_last(joined_grad, back_project), normed_one, inverse_one
        )
        feed_one = jnp.einsum("lsd,ld->s", tokens, entry_grad_one, precision=HIGH)
        tokens_grad = (
            jnp.einsum("st,ltd->lsd", mixing[0, :, 2:], middle_grad, precision=HIGH)
            + mixing[0, None, :, 0, None] * entry_grad_one[:, None, :]
        )
        outputs_grad.append(tokens_grad)
        mix_grad = mix_grad + jnp.stack(
            [
                jnp.concatenate([feed_one[:, None], gain_one[:, None], route_one], axis=1),
                jnp.concatenate([feed_two[:, None], gain_two[:, None], route_two], axis=1),
            ]
        )
        kept.append(
            (entry_one, attended, entry_two, hidden, joined_grad, grad_one, opened_grad, grad_two)
        )
    stacked = [jnp.concatenate([item[index] for item in kept], axis=0) for index in range(8)]
    rows_grad = lax.psum_scatter(
        make_rows((stacked[0], stacked[1], stacked[2]), (stacked[4], stacked[5], stacked[6])),
        ("ctx", "fsdp"),
        scatter_dimension=0,
        tiled=True,
    )
    reduce_grad = lax.psum_scatter(
        make_down(stacked[3], stacked[7]), ("ctx", "fsdp"), scatter_dimension=0, tiled=True
    )
    local_squares = jnp.sum(rows_grad * rows_grad) + jnp.sum(reduce_grad * reduce_grad)
    squares, mix_total = lax.psum((local_squares, mix_grad), ("ctx", "fsdp"))
    norm = jnp.sqrt(squares + jnp.sum(mix_total * mix_total))
    factor = THRESHOLD / jnp.maximum(norm, THRESHOLD)
    width_project = w_project.shape[1]
    width_output = w_output.shape[1]
    project_grad = rows_grad[:, :width_project]
    output_grad = rows_grad[:, width_project : width_project + width_output]
    expand_grad = rows_grad[:, width_project + width_output :]
    mix_new = adam(mixing, mix_total, first_mixing, second_mixing, factor, RATE_MIXING, 0.0)
    proj_new = adam(
        w_project, project_grad, first_project, second_project, factor, RATE_MATRIX, DECAY_MATRIX
    )
    outp_new = adam(
        w_output, output_grad, first_output, second_output, factor, RATE_MATRIX, DECAY_MATRIX
    )
    expd_new = adam(
        w_expand, expand_grad, first_expand, second_expand, factor, RATE_MATRIX, DECAY_MATRIX
    )
    redc_new = adam(
        w_reduce, reduce_grad, first_reduce, second_reduce, factor, RATE_MATRIX, DECAY_MATRIX
    )
    fresh = jnp.stack(outputs_new)[:, None]
    backed = jnp.stack(outputs_grad)[:, None]
    return (
        fresh,
        backed,
        norm,
        mix_new[0],
        mix_new[1],
        mix_new[2],
        proj_new[0],
        proj_new[1],
        proj_new[2],
        outp_new[0],
        outp_new[1],
        outp_new[2],
        expd_new[0],
        expd_new[1],
        expd_new[2],
        redc_new[0],
        redc_new[1],
        redc_new[2],
    )


def solution(mesh):
    return jax.shard_map(
        body,
        mesh=mesh,
        in_specs=(
            P(None, "fsdp", "ctx", None, None),
            P(None, "fsdp", "ctx"),
            P(None, "fsdp", "ctx", None, None),
            P(),
            P(("ctx", "fsdp"), None),
            P(("ctx", "fsdp"), None),
            P(("ctx", "fsdp"), None),
            P(("ctx", "fsdp"), None),
            P(),
            P(),
            P(("ctx", "fsdp"), None),
            P(("ctx", "fsdp"), None),
            P(("ctx", "fsdp"), None),
            P(("ctx", "fsdp"), None),
            P(("ctx", "fsdp"), None),
            P(("ctx", "fsdp"), None),
            P(("ctx", "fsdp"), None),
            P(("ctx", "fsdp"), None),
        ),
        out_specs=(
            P(None, "fsdp", "ctx", None, None),
            P(None, "fsdp", "ctx", None, None),
            P(),
            P(),
            P(),
            P(),
            P(("ctx", "fsdp"), None),
            P(("ctx", "fsdp"), None),
            P(("ctx", "fsdp"), None),
            P(("ctx", "fsdp"), None),
            P(("ctx", "fsdp"), None),
            P(("ctx", "fsdp"), None),
            P(("ctx", "fsdp"), None),
            P(("ctx", "fsdp"), None),
            P(("ctx", "fsdp"), None),
            P(("ctx", "fsdp"), None),
            P(("ctx", "fsdp"), None),
            P(("ctx", "fsdp"), None),
        ),
        check_vma=False,
    )
```

profile of v0, /device:TPU:0, one launch (start us, length us, event | category | flops | bytes accessed | tf_op | source)
XLA Modules:
  0.0 5562.2 jit_solution(6128209729614623853)
XLA Ops:
  15.8 203.8 %all-gather.20.cloned.1.call-done = bf16[2048,2560]{1,0:T(8,128)(2,1)} async-done(((bf16[16,2560]{1,0:T(8,128)(2,1)}), bf16[2048,2560]{1,0:T(8,128)(2,1)}) %all-gather.20.cloned.1.call-update) | async-done | bytes 10485776 | tf_op jit(solution)/shard_map/all_gather | solution.py:152
  244.8 47.6 all-gather.32.cloned.1.call-done
  307.6 52.7 all-gather.30.cloned.1.call-done
  371.0 191.9 %all-gather.26.cloned.1.call-done = bf16[2048,2048]{1,0:T(8,128)(2,1)} async-done(((bf16[16,2048]{1,0:T(8,128)(2,1)}), bf16[2048,2048]{1,0:T(8,128)(2,1)}) %all-gather.26.cloned.1.call-update) | async-done | bytes 8388624 | tf_op jit(solution)/shard_map/all_gather | solution.py:153
  577.7 213.4 %all-gather.46.cloned.1.call-done = bf16[128,44,2048]{2,1,0:T(8,128)(2,1)} async-done(((bf16[1,44,2048]{2,1,0:T(8,128)(2,1)}), bf16[128,44,2048]{2,1,0:T(8,128)(2,1)}) %all-gather.46.cloned.1.call-update) | async-done | bytes 23068688 | tf_op jit(solution)/shard_map/all_gather | solution.py:155
  791.1 30.3 reshape.430
  821.5 230.4 %all-gather.28.cloned.1.call-done = bf16[2048,11264]{1,0:T(8,128)(2,1)} async-done(((bf16[16,11264]{1,0:T(8,128)(2,1)}), bf16[2048,11264]{1,0:T(8,128)(2,1)}) %all-gather.28.cloned.1.call-update) | async-done | bytes 46137360 | tf_op jit(solution)/shard_map/all_gather | solution.py:154
  1051.9 18.2 fusion.183
  1087.7 33.6 all-gather.22.cloned.1.call-done
  1123.7 64.9 %all-gather.24.cloned.1.call-done = bf16[2048,256]{1,0:T(8,128)(2,1)} async-done(((bf16[64,256]{1,0:T(8,128)(2,1)}), bf16[2048,256]{1,0:T(8,128)(2,1)}) %all-gather.24.cloned.1.call-update) | async-done | bytes 1048592 | tf_op jit(solution)/shard_map/all_gather | solution.py:181
  1216.9 18.8 fusion.179
  1262.6 153.1 %all-gather.50.cloned.1.call-done = bf16[128,44,2048]{2,1,0:T(8,128)(2,1)} async-done(((bf16[1,44,2048]{2,1,0:T(8,128)(2,1)}), bf16[128,44,2048]{2,1,0:T(8,128)(2,1)}) %all-gather.50.cloned.1.call-update) | async-done | bytes 23068688 | tf_op jit(solution)/shard_map/all_gather | solution.py:211
  1415.7 30.2 reshape.434
  1458.6 185.3 %all-gather.48.cloned.1.call-done = bf16[128,44,2048]{2,1,0:T(8,128)(2,1)} async-done(((bf16[1,44,2048]{2,1,0:T(8,128)(2,1)}), bf16[128,44,2048]{2,1,0:T(8,128)(2,1)}) %all-gather.48.cloned.1.call-update) | async-done | bytes 23068688 | tf_op jit(solution)/shard_map/all_gather | solution.py:211
  1643.8 30.3 reshape.432
  1687.0 217.6 %all-gather.40.cloned.1.call-done = bf16[2048,11264]{1,0:T(8,128)(2,1)} async-done(((bf16[16,11264]{1,0:T(8,128)(2,1)}), bf16[2048,11264]{1,0:T(8,128)(2,1)}) %all-gather.40.cloned.1.call-update) | async-done | bytes 46137360 | tf_op jit(solution)/shard_map/all_gather | solution.py:210
  1904.6 20.2 fusion.167
  1933.0 176.2 %all-gather.42.cloned.1.call-done = bf16[2048,2048]{1,0:T(8,128)(2,1)} async-done(((bf16[16,2048]{1,0:T(8,128)(2,1)}), bf16[2048,2048]{1,0:T(8,128)(2,1)}) %all-gather.42.cloned.1.call-update) | async-done | bytes 8388624 | tf_op jit(solution)/shard_map/all_gather | solution.py:209
  2151.6 218.6 %all-gather.34.cloned.1.call-done = bf16[2048,11264]{1,0:T(8,128)(2,1)} async-done(((bf16[16,11264]{1,0:T(8,128)(2,1)}), bf16[2048,11264]{1,0:T(8,128)(2,1)}) %all-gather.34.cloned.1.call-update) | async-done | bytes 46137360 | tf_op jit(solution)/shard_map/all_gather | solution.py:210
  2370.3 20.1 fusion.165
  2399.7 174.7 %all-gather.36.cloned.1.call-done = bf16[2048,2048]{1,0:T(8,128)(2,1)} async-done(((bf16[16,2048]{1,0:T(8,128)(2,1)}), bf16[2048,2048]{1,0:T(8,128)(2,1)}) %all-gather.36.cloned.1.call-update) | async-done | bytes 8388624 | tf_op jit(solution)/shard_map/all_gather | solution.py:209
  2636.4 33.7 fusion.21
  2706.2 53.9 reduce-scatter.22.cloned.1.call-done
  2761.5 180.7 %reduce-scatter.18.cloned.1.call-done = bf16[64,256]{1,0:T(8,128)(2,1)} async-done(((bf16[2048,256]{1,0:T(8,128)(2,1)}), bf16[64,256]{1,0:T(8,128)(2,1)}) %reduce-scatter.18.cloned.1.call-update) | async-done | bytes 32784
  2943.7 180.6 %reduce-scatter.24.cloned.1.call-done = bf16[64,256]{1,0:T(8,128)(2,1)} async-done(((bf16[2048,256]{1,0:T(8,128)(2,1)}), bf16[64,256]{1,0:T(8,128)(2,1)}) %reduce-scatter.24.cloned.1.call-update) | async-done | bytes 32784 | tf_op jit(solution)/shard_map/reduce_scatter | solution.py:277
  3125.1 181.4 %reduce-scatter.20.cloned.1.call-done = bf16[64,256]{1,0:T(8,128)(2,1)} async-done(((bf16[2048,256]{1,0:T(8,128)(2,1)}), bf16[64,256]{1,0:T(8,128)(2,1)}) %reduce-scatter.20.cloned.1.call-update) | async-done | bytes 32784 | tf_op jit(solution)/shard_map/reduce_scatter | solution.py:277
  3316.0 84.9 %pad_maximum_fusion = f32[2048,15872]{1,0:T(8,128)} fusion(f32[2048,11264]{1,0:T(8,128)} %fusion.21, f32[2048,2048]{1,0:T(8,128)} %fusion.81, f32[2048,2560]{1,0:T(8,128)} %fusion.74), kind=kLoop, calls=%fused_computation | loop fusion | flops 65011712 | bytes 260046848 | tf_op jit(solution)/shard_map/concatenate | solution.py:79
  3420.4 882.7 %fusion = f32[48,2048]{1,0:T(8,128)S(1)} fusion(f32[5632,2048]{1,0:T(8,128)} %fusion.63), kind=kCustom, calls=%all-reduce-scatter | all-reduce-scatter fusion | flops 12582913 | bytes 46530560
  4368.4 33.2 collective-permute-start.2
  4424.7 31.1 concatenate.126
  4542.3 915.8 %reduce-scatter.16.cloned.1.call-done = f32[16,15872]{1,0:T(8,128)} async-done(((f32[2048,15872]{1,0:T(8,128)}), f32[16,15872]{1,0:T(8,128)}) %reduce-scatter.16.cloned.1.call-update) | async-done | bytes 1015824 | tf_op jit(solution)/shard_map/reduce_scatter | solution.py:311
  5466.7 75.2 %all-reduce.2 = (f32[]{:T(128)}, f32[2,4,6]{2,1,0:T(4,128)S(1)}) all-reduce(f32[]{:T(128)S(6)} %add.237, f32[2,4,6]{2,1,0:T(4,128)S(1)} %maximum_add_fusion), channel_id=1, replica_groups=mesh['ctx'=32,'fsdp'=4] {'ctx','fsdp'}, use_global_device_ids=true, to_apply=%region_30.31 | all-reduce | flops 49 | bytes 392 | tf_op jit(solution)/shard_map/psum | solution.py:321
  (584 shorter events, 556.1 us)
Async XLA Ops:
  7.2 212.4 %all-gather.20.cloned.1.call-start = ((), (), s32[]{:S(2)}) async-start(), calls=%async_computation.5 | async-start | bytes 10567680 | tf_op jit(solution)/shard_map/all_gather | solution.py:152
  8.8 283.6 %all-gather.32.cloned.1.call-start = ((), (), s32[]{:S(2)}) async-start(), calls=%async_computation.11 | async-start | bytes 1081344 | tf_op jit(solution)/shard_map/all_gather | solution.py:181
  226.6 133.7 %all-gather.30.cloned.1.call-start = ((), (), s32[]{:S(2)}) async-start(), calls=%async_computation.10 | async-start | bytes 1081344 | tf_op jit(solution)/shard_map/all_gather | solution.py:182
  227.4 335.6 %all-gather.26.cloned.1.call-start = ((), (), s32[]{:S(2)}) async-start(), calls=%async_computation.8 | async-start | bytes 8454144 | tf_op jit(solution)/shard_map/all_gather | solution.py:153
  228.1 563.0 %all-gather.46.cloned.1.call-start = ((), (), s32[]{:S(2)}) async-start(), calls=%async_computation.19 | async-start | bytes 25362432 | tf_op jit(solution)/shard_map/all_gather | solution.py:155
  228.9 823.0 %all-gather.28.cloned.1.call-start = ((), (), s32[]{:S(2)}) async-start(), calls=%async_computation.9 | async-start | bytes 46497792 | tf_op jit(solution)/shard_map/all_gather | solution.py:154
  229.7 891.6 %all-gather.22.cloned.1.call-start = ((), (), s32[]{:S(2)}) async-start(), calls=%async_computation.6 | async-start | bytes 1081344 | tf_op jit(solution)/shard_map/all_gather | solution.py:182
  240.6 948.1 %all-gather.24.cloned.1.call-start = ((), (), s32[]{:S(2)}) async-start(), calls=%async_computation.7 | async-start | bytes 1081344 | tf_op jit(solution)/shard_map/all_gather | solution.py:181
  244.5 1171.2 %all-gather.50.cloned.1.call-start = ((), (), s32[]{:S(2)}) async-start(), calls=%async_computation.21 | async-start | bytes 25362432 | tf_op jit(solution)/shard_map/all_gather | solution.py:211
  1086.3 557.5 %all-gather.48.cloned.1.call-start = ((), (), s32[]{:S(2)}) async-start(), calls=%async_computation.20 | async-start | bytes 25362432 | tf_op jit(solution)/shard_map/all_gather | solution.py:211
  1252.1 652.6 %all-gather.40.cloned.1.call-start = ((), (), s32[]{:S(2)}) async-start(), calls=%async_computation.15 | async-start | bytes 46497792 | tf_op jit(solution)/shard_map/all_gather | solution.py:210
  1252.8 856.4 %all-gather.42.cloned.1.call-start = ((), (), s32[]{:S(2)}) async-start(), calls=%async_computation.16 | async-start | bytes 8454144 | tf_op jit(solution)/shard_map/all_gather | solution.py:209
  1253.4 1116.9 %all-gather.34.cloned.1.call-start = ((), (), s32[]{:S(2)}) async-start(), calls=%async_computation.12 | async-start | bytes 46497792 | tf_op jit(solution)/shard_map/all_gather | solution.py:210
  1254.1 1320.3 %all-gather.36.cloned.1.call-start = ((), (), s32[]{:S(2)}) async-start(), calls=%async_computation.13 | async-start | bytes 8454144 | tf_op jit(solution)/shard_map/all_gather | solution.py:209
  1262.1 1498.0 %reduce-scatter.22.cloned.1.call-start = ((), (), s32[]{:S(2)}) async-start(), calls=%async_computation.24 | async-start | bytes 1081344
  2399.7 542.6 %reduce-scatter.18.cloned.1.call-start = ((), (), s32[]{:S(2)}) async-start(), calls=%async_computation.22 | async-start | bytes 1081344
  2613.5 510.8 %reduce-scatter.24.cloned.1.call-start = ((), (), s32[]{:S(2)}) async-start(), calls=%async_computation.25 | async-start | bytes 1081344 | tf_op jit(solution)/shard_map/reduce_scatter | solution.py:277
  2624.4 682.1 %reduce-scatter.20.cloned.1.call-start = ((), (), s32[]{:S(2)}) async-start(), calls=%async_computation.23 | async-start | bytes 1081344 | tf_op jit(solution)/shard_map/reduce_scatter | solution.py:277
  2635.0 1871.7 %all-gather.44.cloned.1.call-start = ((), (), s32[]{:S(2)}) async-start(), calls=%async_computation.17 | async-start | bytes 10567680 | tf_op jit(solution)/shard_map/all_gather | solution.py:208
  2635.7 1883.8 %all-gather.38.cloned.1.call-start = ((), (), s32[]{:S(2)}) async-start(), calls=%async_computation.14 | async-start | bytes 10567680 | tf_op jit(solution)/shard_map/all_gather | solution.py:208
  2636.3 2821.8 %reduce-scatter.16.cloned.1.call-start = ((), (), s32[]{:S(2)}) async-start(), calls=%async_computation.18 | async-start | bytes 131039232 | tf_op jit(solution)/shard_map/reduce_scatter | solution.py:311
  4303.2 31.3 collective-permute-start.10
  4320.1 35.9 collective-permute-start.9
  4321.5 40.2 collective-permute-start.8
  4322.8 45.5 collective-permute-start.7
  4324.2 77.4 %collective-permute-start.6 = (f32[48,2048]{1,0:T(8,128)S(1)}, f32[48,2048]{1,0:T(8,128)S(1)}, u32[]{:S(2)}, u32[]{:S(2)}) collective-permute-start(f32[48,2048]{1,0:T(8,128)S(1)} %fusion), channel_id=1, source_target_pairs={{0,7},{1,8},{2,9},{3,10},{4,11},{5,12},{6,13},{7,14},{8,15},{9,16}... | collective-permute-start | bytes 1179656
  4334.5 69.3 %collective-permute-start.5 = (f32[48,2048]{1,0:T(8,128)S(1)}, f32[48,2048]{1,0:T(8,128)S(1)}, u32[]{:S(2)}, u32[]{:S(2)}) collective-permute-start(f32[48,2048]{1,0:T(8,128)S(1)} %fusion), channel_id=1, source_target_pairs={{0,6},{1,7},{2,8},{3,9},{4,10},{5,11},{6,12},{7,13},{8,14},{9,15},... | collective-permute-start | bytes 1179656
  4355.9 58.4 %collective-permute-start.4 = (f32[48,2048]{1,0:T(8,128)S(1)}, f32[48,2048]{1,0:T(8,128)S(1)}, u32[]{:S(2)}, u32[]{:S(2)}) collective-permute-start(f32[48,2048]{1,0:T(8,128)S(1)} %fusion), channel_id=1, source_target_pairs={{0,5},{1,6},{2,7},{3,8},{4,9},{5,10},{6,11},{7,12},{8,13},{9,14},{... | collective-permute-start | bytes 1179656
  4361.7 52.7 collective-permute-start.3
  4368.4 46.0 collective-permute-start.2
  4401.6 22.4 collective-permute-start.1
  4403.8 20.9 collective-permute-start
  (163 other events, 14854.6 us)
Sparse Core Ops, SparseCore 0:
  10.3 209.1 all-gather.19
  226.7 65.5 all-gather.31
  296.0 64.2 all-gather.29
  362.4 200.4 all-gather.25
  565.1 226.0 all-gather.45
  793.3 258.5 all-gather.27
  1055.0 66.2 all-gather.21
  1124.4 64.2 all-gather.23
  1191.0 224.6 all-gather.49
  1417.8 225.9 all-gather.47
  1646.1 258.4 all-gather.39
  1906.8 202.3 all-gather.41
  2111.5 258.6 all-gather.33
  2372.4 202.0 all-gather.35
  2576.6 183.4 reduce-scatter.21
  2762.4 179.7 reduce-scatter.17
  2944.5 179.7 reduce-scatter.23
  3126.6 179.7 reduce-scatter.19
  3308.8 207.4 all-gather.43
  3518.5 215.9 all-gather.37
  3736.9 1721.1 reduce-scatter.15
where the time goes:
time: 5580 us; the launch traced here: 5560 us
  waiting for transfers between devices  3690 us (66%)
  blocking collectives  958 us (17%)
  matrix products  468 us (8%)
  local copies, waits for them, and re-layouts  181 us (3%)
  other arithmetic  158 us (3%)
  starting transfers between devices  87.7 us (2%)
    reduce_scatter x1, waiting for transfers between devices, body(): lax.psum_scatter(make_rows((stacked[0], stacked[1], stacked[2]), (stacked...  916 us
    unnamed x1, blocking collectives  883 us
    all_gather x2, waiting for transfers between devices, body(): lax.all_gather(held[2], ('ctx', 'fsdp'), axis=0, tiled=True)  436 us
    reduce_scatter x2, waiting for transfers between devices, body(): lax.psum_scatter(value_term.reshape(length, KV * HD).astype(jnp.bfloat16)...  362 us
    all_gather x2, waiting for transfers between devices, body(): lax.all_gather(held[1], ('ctx', 'fsdp'), axis=0, tiled=True)  351 us
    all_gather x2, waiting for transfers between devices, body(): lax.all_gather(held[3], ('ctx', 'fsdp'), axis=0, tiled=True)  338 us
    unnamed x34, waiting for transfers between devices  248 us
    all_gather x1, waiting for transfers between devices, body(): lax.all_gather(shard_expand, ('ctx', 'fsdp'), axis=0, tiled=True)  230 us
  transfers between devices with their start and end apart: 32, of which 20 were waited for; matrix products, arithmetic and copies ran while one was open for 29% of the time, Pallas kernels for 0%

commit v1 on v0

v1 whole, which is shorter than its diff:
```python
import functools
import math

import jax
import jax.numpy as jnp
from jax import lax
from jax.experimental import pallas as pl
from jax.experimental.pallas import tpu as pltpu
from jax.sharding import PartitionSpec as P

H = 32
FF = 5632
STEP = 10
THETA_BASE = 10000.0
BETA_ONE = 0.9
BETA_TWO = 0.95
ADAM_EPS = 1e-08
RATE_MATRIX = 0.06
RATE_MIXING = 0.5
DECAY_MATRIX = 0.1
THRESHOLD = 1.0


MESH = pl.DeviceIdType.MESH


def place():
    ctx = lax.axis_index("ctx")
    fsdp = lax.axis_index("fsdp")
    return (2 * (ctx // 16) + fsdp // 2, (ctx // 4) % 4, ctx % 4, fsdp % 2)


def ident(x, y, z, c):
    return ((x // 2) * 16 + y * 4 + z, (x % 2) * 2 + c)


def moved(spot, axis, step):
    spot = list(spot)
    spot[axis] = (spot[axis] + step + 4) % 4
    return tuple(spot)


def neighbours(spot):
    x, y, z, c = spot
    out = [(x, y, z, 1 - c)]
    for axis in range(3):
        out += [moved(spot, axis, 1), moved(spot, axis, -1)]
    return out


def meet(spot):
    barrier = pltpu.get_barrier_semaphore()
    for other in neighbours(spot):
        pl.semaphore_signal(barrier, inc=1, device_id=ident(*other), device_id_type=MESH)
    pl.semaphore_wait(barrier, 7)


def box(spot, known, axis=None, at=None):
    x, y, z, c = spot
    place = [x, y, z]
    if axis is not None:
        place[axis] = at
    index = []
    for d in range(3):
        whole = d in known
        if d == 0:
            xs = (slice(None), slice(None)) if whole else (place[0] // 2, place[0] % 2)
        elif whole:
            index.append(slice(None))
        else:
            index.append(place[d])
    return (xs[0], index[0], index[1], xs[1])


def thirds(tiles):
    cuts = [0, (tiles + 2) // 3, (tiles + 2) // 3 + (tiles + 1) // 3, tiles]
    out = []
    for a, b in zip(cuts[:-1], cuts[1:]):
        mid = a + (b - a + 1) // 2
        out.append((a * 128, mid * 128, b * 128))
    return out


def gather_kernel(n, *refs):
    shards = refs[:n]
    outs = refs[n : 2 * n]
    own_sem, send, recv, csend, crecv = refs[2 * n :]
    spot = place()
    x, y, z, c = spot
    sibling = ident(x, y, z, 1 - c)
    pieces = [thirds(o.shape[-1] // 128) for o in outs]
    local = []
    for w in range(n):
        copy = pltpu.make_async_copy(shards[w], outs[w].at[x // 2, y, z, x % 2, c], own_sem.at[w])
        copy.start()
        local.append(copy)
    meet(spot)
    cross = []

    def core_copy(w, slot, index, a, b):
        view = outs[w].at[index + (c, slice(None), slice(a, b))]
        copy = pltpu.make_async_remote_copy(
            view, view, csend.at[w, slot], crecv.at[w, slot], device_id=sibling, device_id_type=MESH
        )
        copy.start()
        cross.append(copy)

    def ring_copy(w, p, k, j, index, a, b, to):
        view = outs[w].at[index + (c, slice(None), slice(a, b))]
        copy = pltpu.make_async_remote_copy(
            view, view, send.at[w, p, k, j], recv.at[w, p, k, j], device_id=ident(*to), device_id_type=MESH
        )
        copy.start()
        return copy

    for w in range(n):
        local[w].wait()
        core_copy(w, 0, (x // 2, y, z, x % 2), 0, outs[w].shape[-1])
    ring = {}
    for k in range(3):
        for w in range(n):
            for p in range(3):
                order = (p, (p + 1) % 3, (p + 2) % 3)
                axis, known = order[k], order[:k]
                a, m, b = pieces[w][p]
                if k:
                    for j in (2, 3):
                        ring[w, p, k - 1, j].wait_recv()
                    prev = order[k - 1]
                    core_copy(w, 3 * (3 * p + k - 1) + 3, box(spot, order[: k - 1], prev, (spot[prev] + 2) % 4), a, b)
                mine = box(spot, known)
                ring[w, p, k, 0] = ring_copy(w, p, k, 0, mine, a, b, moved(spot, axis, 1))
                ring[w, p, k, 1] = ring_copy(w, p, k, 1, mine, a, b, moved(spot, axis, -1))
        for w in range(n):
            for p in range(3):
                order = (p, (p + 1) % 3, (p + 2) % 3)
                axis, known = order[k], order[:k]
                a, m, b = pieces[w][p]
                ring[w, p, k, 0].wait_recv()
                left = box(spot, known, axis, (spot[axis] + 3) % 4)
                ring[w, p, k, 2] = ring_copy(w, p, k, 2, left, a, m, moved(spot, axis, 1))
                core_copy(w, 3 * (3 * p + k) + 1, left, a, b)
                ring[w, p, k, 1].wait_recv()
                right = box(spot, known, axis, (spot[axis] + 1) % 4)
                ring[w, p, k, 3] = ring_copy(w, p, k, 3, right, m, b, moved(spot, axis, -1))
                core_copy(w, 3 * (3 * p + k) + 2, right, a, b)
    for w in range(n):
        for p in range(3):
            order = (p, (p + 1) % 3, (p + 2) % 3)
            a, m, b = pieces[w][p]
            for j in (2, 3):
                ring[w, p, 2, j].wait_recv()
            prev = order[2]
            core_copy(w, 3 * (3 * p + 2) + 3, box(spot, order[:2], prev, (spot[prev] + 2) % 4), a, b)
    for copy in ring.values():
        copy.wait_send()
    for copy in cross:
        copy.wait()


def gather(shards, collective_id):
    n = len(shards)
    return pl.pallas_call(
        functools.partial(gather_kernel, n),
        out_shape=[jax.ShapeDtypeStruct((2, 4, 4, 2, 2) + s.shape, s.dtype) for s in shards],
        in_specs=[pl.BlockSpec(memory_space=pl.ANY)] * n,
        out_specs=[pl.BlockSpec(memory_space=pl.ANY)] * n,
        scratch_shapes=[
            pltpu.SemaphoreType.DMA((n,)),
            pltpu.SemaphoreType.DMA((n, 3, 3, 4)),
            pltpu.SemaphoreType.DMA((n, 3, 3, 4)),
            pltpu.SemaphoreType.DMA((n, 28)),
            pltpu.SemaphoreType.DMA((n, 28)),
        ],
        compiler_params=pltpu.CompilerParams(collective_id=collective_id, has_side_effects=True),
    )(*shards)


W = 512
HALF = 256
UNITS = 45
CHUNKS = 15
SLOTS = 3
STAGES = 6
COLS = 2048 + 12288 + 2048 + 2560


def unit_spot(u):
    early = u // 12
    early = 1 - (1 // (1 + early))
    left = (1 - early) * (u // 4) + early * (3 + u // 36 + u // 40)
    column = (1 - early) * ((u % 4) * W) + early * (2048 + (u - 12) * W)
    return left, pl.multiple_of(column, W)


def scatter_kernel(lhs, rhs, mix, grads, total, left, right, acc1, acc2,
                   sa, ra, sb, rb, sc, rc, sd, rd, se, re, sf, rf, vsend, vrecv, out,
                   send_sem, recv_sem, free_sem, local_sem, side_send, side_recv, out_sem, v_send_sem, v_recv_sem):
    spot = place()
    x, y, z, c = spot
    pos = (x, y, z)
    sibling = (x, y, z, 1 - c)
    barrier = pltpu.get_barrier_semaphore()
    others = [sibling] + [moved(spot, axis, step) for axis in range(3) for step in (1, 2, 3)]
    for other in others:
        pl.semaphore_signal(barrier, inc=1, device_id=ident(*other), device_id_type=MESH)
    pl.semaphore_wait(barrier, len(others))

    parts = (((0, 3), (0, 2048)), ((3, 4), (2048, 14336)), ((4, 6), (14336, COLS)))
    moves = []
    for j, ((l0, l1), (c0, c1)) in enumerate(parts):
        own = [
            pltpu.make_async_copy(lhs.at[c, l0:l1], left.at[l0:l1, :, :, :, :, 0:128], local_sem.at[j, 0]),
            pltpu.make_async_copy(rhs.at[:, c0:c1], right.at[0:128, c0:c1], local_sem.at[j, 1]),
        ]
        far = [
            pltpu.make_async_remote_copy(
                lhs.at[1 - c, l0:l1], left.at[l0:l1, :, :, :, :, 128:256], side_send.at[j, 0], side_recv.at[j, 0],
                device_id=ident(*sibling), device_id_type=MESH),
            pltpu.make_async_remote_copy(
                rhs.at[:, c0:c1], right.at[128:256, c0:c1], side_send.at[j, 1], side_recv.at[j, 1],
                device_id=ident(*sibling), device_id_type=MESH),
        ]
        for copy in own + far:
            copy.start()
        moves.append((own, far))

    def arrive(j):
        for copy in moves[j][0]:
            copy.wait()
        for copy in moves[j][1]:
            copy.wait_recv()

    arrive(0)

    sends = (sa, sb, sc, sd, se, sf)
    recvs = (ra, rb, rc, rd, re, rf)

    def hop(stage, p, d, slot):
        axis = (p + stage // 2) % 3
        return pltpu.make_async_remote_copy(
            sends[stage].at[p, d, slot], recvs[stage].at[p, d, slot],
            send_sem.at[stage, p, d, slot], recv_sem.at[stage, p, d, slot],
            device_id=ident(*moved(spot, axis, 1 - 2 * d)), device_id_type=MESH)

    def before_send(stage, p, q):
        @pl.when(q >= SLOTS)
        def _():
            for d in (0, 1):
                hop(stage, p, d, q % SLOTS).wait_send()
                pl.semaphore_wait(free_sem.at[stage, p, d], 1)

    def give_back(stage, p, q):
        @pl.when(q < CHUNKS - SLOTS)
        def _():
            axis = (p + stage // 2) % 3
            for d in (0, 1):
                pl.semaphore_signal(free_sem.at[stage, p, d], inc=1,
                                    device_id=ident(*moved(spot, axis, 2 * d - 1)), device_id_type=MESH)

    def go(stage, p, q):
        for d in (0, 1):
            hop(stage, p, d, q % SLOTS).start()

    def come(stage, p, q):
        for d in (0, 1):
            hop(stage, p, d, q % SLOTS).wait_recv()

    def rows(p, l, a):
        if p == 0:
            got = left[l, a]
        elif p == 1:
            got = left[l, :, a]
        else:
            got = left[l, :, :, a]
        return got.reshape(256, 256)

    def product(p, q, a, lo, hi):
        l, column = unit_spot(3 * q + p)
        return jnp.dot(rows(p, l, a), right[:, pl.ds(pl.multiple_of(column + lo, HALF), hi - lo)],
                       preferred_element_type=jnp.float32)

    def at(p, step):
        return (pos[p] + step + 4) % 4

    bf = jnp.bfloat16
    f32 = jnp.float32

    def stage1(q):
        s = q % SLOTS
        for p in range(3):
            before_send(0, p, q)
            for d in (0, 1):
                sa[p, d, s] = product(p, q, at(p, 2), d * HALF, d * HALF + HALF).astype(bf)
            go(0, p, q)

    def stage2(q):
        s = q % SLOTS
        for p in range(3):
            before_send(1, p, q)
            come(0, p, q)
            for d in (0, 1):
                lo = d * HALF
                near = at(p, 1 - 2 * d)
                sb[p, d, s, :, lo : lo + HALF] = (
                    product(p, q, near, lo, lo + HALF) + ra[p, d, s].astype(f32)).astype(bf)
                other = HALF - lo
                sb[p, d, s, :, other : other + HALF] = product(p, q, near, other, other + HALF).astype(bf)
            give_back(0, p, q)
            go(1, p, q)

    def part(p, ref, b):
        return ref.at[:, b] if p == 1 else ref.at[b]

    def stage3(q):
        s = q % SLOTS
        for p in range(3):
            come(1, p, q)
            for lo in (0, HALF):
                both = (product(p, q, pos[p], lo, lo + HALF)
                        + rb[p, 0, s, :, lo : lo + HALF].astype(f32) + rb[p, 1, s, :, lo : lo + HALF].astype(f32))
                acc1[p, s, :, :, :, lo : lo + HALF] = both.reshape(4, 4, 16, HALF)
            give_back(1, p, q)
            before_send(2, p, q)
            ahead = at((p + 1) % 3, 2)
            for d in (0, 1):
                sc[p, d, s] = part(p, acc1.at[p, s], ahead)[:, :, d * HALF : d * HALF + HALF].astype(bf)
            go(2, p, q)

    def stage4(q):
        s = q % SLOTS
        for p in range(3):
            before_send(3, p, q)
            come(2, p, q)
            for d in (0, 1):
                lo = d * HALF
                other = HALF - lo
                mine = part(p, acc1.at[p, s], at((p + 1) % 3, 1 - 2 * d))
                sd[p, d, s, :, :, lo : lo + HALF] = (
                    mine[:, :, lo : lo + HALF] + rc[p, d, s].astype(f32)).astype(bf)
                sd[p, d, s, :, :, other : other + HALF] = mine[:, :, other : other + HALF].astype(bf)
            give_back(2, p, q)
            go(3, p, q)

    def stage5(q):
        s = q % SLOTS
        for p in range(3):
            come(3, p, q)
            acc2[p, s] = (part(p, acc1.at[p, s], pos[(p + 1) % 3])[...]
                          + rd[p, 0, s].astype(f32) + rd[p, 1, s].astype(f32))
            give_back(3, p, q)
            before_send(4, p, q)
            ahead = at((p + 2) % 3, 2)
            for d in (0, 1):
                se[p, d, s] = acc2[p, s, ahead, :, d * HALF : d * HALF + HALF].astype(bf)
            go(4, p, q)

    def stage6(q):
        s = q % SLOTS
        for p in range(3):
            before_send(5, p, q)
            come(4, p, q)
            for d in (0, 1):
                lo = d * HALF
                other = HALF - lo
                near = at((p + 2) % 3, 1 - 2 * d)
                sf[p, d, s, :, lo : lo + HALF] = (
                    acc2[p, s, near, :, lo : lo + HALF] + re[p, d, s].astype(f32)).astype(bf)
                sf[p, d, s, :, other : other + HALF] = acc2[p, s, near, :, other : other + HALF].astype(bf)
            give_back(4, p, q)
            go(5, p, q)

    def stage7(q):
        s = q % SLOTS
        for p in range(3):
            come(5, p, q)
            out[3 * q + p] = (acc2[p, s, pos[(p + 2) % 3]]
                              + rf[p, 0, s].astype(f32) + rf[p, 1, s].astype(f32))
            give_back(5, p, q)

    def step(t, carry):
        @pl.when(t == 4)
        def _():
            arrive(1)

        @pl.when(t == 12)
        def _():
            arrive(2)

        for lag, stage in enumerate((stage1, stage2, stage3, stage4, stage5, stage6, stage7)):
            @pl.when((t >= lag) & (t < CHUNKS + lag))
            def _(stage=stage, lag=lag):
                stage(t - lag)
        return carry

    lax.fori_loop(0, CHUNKS + 6, step, 0)

    def tail(q, carry):
        for stage in range(STAGES):
            for p in range(3):
                for d in (0, 1):
                    hop(stage, p, d, q % SLOTS).wait_send()
        return carry

    lax.fori_loop(CHUNKS - SLOTS, CHUNKS, tail, 0)
    for own, far in moves:
        for copy in far:
            copy.wait_send()

    write = pltpu.make_async_copy(out, grads, out_sem)
    write.start()

    def squares(u, carry):
        g = out[u]
        return carry + g * g

    summed = lax.fori_loop(0, UNITS, squares, jnp.zeros((16, W), f32))
    lanes = jnp.sum(summed, axis=0, keepdims=True)
    lanes = lanes[:, 0:128] + lanes[:, 128:256] + lanes[:, 256:384] + lanes[:, 384:512]
    vector = mix[...] + jnp.where(lax.broadcasted_iota(jnp.int32, (8, 128), 0) == 7, lanes, 0.0)
    for phase in range(4):
        vsend[phase] = vector
        if phase == 0:
            targets = [(0, sibling)]
        else:
            targets = [(step - 1, moved(spot, phase - 1, step)) for step in (1, 2, 3)]
        copies = [
            pltpu.make_async_remote_copy(
                vsend.at[phase], vrecv.at[phase, k], v_send_sem.at[phase, k], v_recv_sem.at[phase, k],
                device_id=ident(*to), device_id_type=MESH)
            for k, to in targets
        ]
        for copy in copies:
            copy.start()
        for copy in copies:
            copy.wait()
        for k, _ in targets:
            vector = vector + vrecv[phase, k]
    total[...] = vector
    write.wait()


def scatter(lhs, rhs, mix, collective_id):
    bf = jnp.bfloat16
    f32 = jnp.float32
    pair = lambda shape: [pltpu.VMEM((3, 2, SLOTS) + shape, bf)] * 2
    return pl.pallas_call(
        scatter_kernel,
        out_shape=[jax.ShapeDtypeStruct((UNITS, 16, W), f32), jax.ShapeDtypeStruct((8, 128), f32)],
        in_specs=[pl.BlockSpec(memory_space=pl.ANY)] * 2 + [pl.BlockSpec(memory_space=pltpu.VMEM)],
        out_specs=[pl.BlockSpec(memory_space=pl.ANY), pl.BlockSpec(memory_space=pltpu.VMEM)],
        scratch_shapes=[
            pltpu.VMEM((6, 4, 4, 4, 16, 256), bf),
            pltpu.VMEM((256, COLS), bf),
            pltpu.VMEM((3, SLOTS, 4, 4, 16, W), f32),
            pltpu.VMEM((3, SLOTS, 4, 16, W), f32),
            *pair((256, HALF)),
            *pair((256, W)),
            *pair((4, 16, HALF)),
            *pair((4, 16, W)),
            *pair((16, HALF)),
            *pair((16, W)),
            pltpu.VMEM((4, 8, 128), f32),
            pltpu.VMEM((4, 3, 8, 128), f32),
            pltpu.VMEM((UNITS, 16, W), f32),
            pltpu.SemaphoreType.DMA((STAGES, 3, 2, SLOTS)),
            pltpu.SemaphoreType.DMA((STAGES, 3, 2, SLOTS)),
            pltpu.SemaphoreType.REGULAR((STAGES, 3, 2)),
            pltpu.SemaphoreType.DMA((3, 2)),
            pltpu.SemaphoreType.DMA((3, 2)),
            pltpu.SemaphoreType.DMA((3, 2)),
            pltpu.SemaphoreType.DMA,
            pltpu.SemaphoreType.DMA((4, 3)),
            pltpu.SemaphoreType.DMA((4, 3)),
        ],
        compiler_params=pltpu.CompilerParams(
            collective_id=collective_id, has_side_effects=True, vmem_limit_bytes=60 * 1024 * 1024),
    )(lhs, rhs, mix)


def kv_meet(spot):
    barrier = pltpu.get_barrier_semaphore()
    others = [moved(spot, 0, 2)] + [moved(spot, axis, step) for axis in (1, 2) for step in (1, -1)]
    for other in others:
        pl.semaphore_signal(barrier, inc=1, device_id=ident(*other), device_id_type=MESH)
    pl.semaphore_wait(barrier, len(others))


def kv_gather_kernel(shard, whole, own_sem, send, recv):
    spot = place()
    x, y, z, c = spot
    xh = x // 2
    own = pltpu.make_async_copy(shard, whole.at[:, xh, y, z], own_sem)
    own.start()
    kv_meet(spot)

    def copy(p, j, src, dst, to):
        made = pltpu.make_async_remote_copy(
            src, dst, send.at[p, j], recv.at[p, j], device_id=ident(*to), device_id_type=MESH)
        made.start()
        return made

    cols = [slice(0, 256), slice(256, 512)]
    made = {}
    for p in range(2):
        made[p, 0] = copy(p, 0, shard.at[:, :, cols[p]], whole.at[:, xh, y, z, :, cols[p]], moved(spot, 0, 2))
    own.wait()
    for k in range(2):
        for p in range(2):
            axis = (1, 2)[(p + k) % 2]
            if k == 0:
                made[p, 0].wait_recv()
                view = whole.at[:, :, y, z, :, cols[p]]
            else:
                made[p, 3].wait_recv()
                made[p, 4].wait_recv()
                view = whole.at[:, :, :, z, :, cols[p]] if axis == 2 else whole.at[:, :, y, :, :, cols[p]]
            made[p, 4 * k + 1] = copy(p, 4 * k + 1, view, view, moved(spot, axis, 1))
            made[p, 4 * k + 2] = copy(p, 4 * k + 2, view, view, moved(spot, axis, -1))
        for p in range(2):
            axis = (1, 2)[(p + k) % 2]
            for d in (0, 1):
                made[p, 4 * k + 1 + d].wait_recv()
                near = (spot[axis] + 3 + 2 * d) % 4
                if k == 0:
                    view = whole.at[d, :, y, near, :, cols[p]] if axis == 2 else whole.at[d, :, near, z, :, cols[p]]
                else:
                    view = whole.at[d, :, :, near, :, cols[p]] if axis == 2 else whole.at[d, :, near, :, :, cols[p]]
                made[p, 4 * k + 3 + d] = copy(p, 4 * k + 3 + d, view, view, moved(spot, axis, 1 - 2 * d))
    for p in range(2):
        made[p, 7].wait_recv()
        made[p, 8].wait_recv()
    for each in made.values():
        each.wait_send()


def kv_gather(shard, collective_id):
    return pl.pallas_call(
        kv_gather_kernel,
        out_shape=jax.ShapeDtypeStruct((2, 2, 4, 4, 64, 512), shard.dtype),
        in_specs=[pl.BlockSpec(memory_space=pltpu.VMEM)],
        out_specs=pl.BlockSpec(memory_space=pltpu.VMEM),
        scratch_shapes=[
            pltpu.SemaphoreType.DMA,
            pltpu.SemaphoreType.DMA((2, 9)),
            pltpu.SemaphoreType.DMA((2, 9)),
        ],
        compiler_params=pltpu.CompilerParams(
            collective_id=collective_id, has_side_effects=True, vmem_limit_bytes=32 * 1024 * 1024),
    )(shard)


def kv_scatter_kernel(terms, got, s1, r1, s2, r2, s3, r3, s4, r4, s5, r5, acc, acc2, send, recv):
    spot = place()
    x, y, z, c = spot
    xh = x // 2
    kv_meet(spot)
    bf, f32 = jnp.bfloat16, jnp.float32
    cols = [slice(0, 256), slice(256, 512)]
    axes = [(2, 1), (1, 2)]

    def copy(stage, p, d, src, dst, to):
        made = pltpu.make_async_remote_copy(
            src, dst, send.at[stage, p, d], recv.at[stage, p, d], device_id=ident(*to), device_id_type=MESH)
        made.start()
        return made

    def block(p, m, at):
        if p == 0:
            return terms[m, :, :, at, :, cols[p]]
        return terms[m, :, at, :, :, cols[p]]

    made = {}
    for p in range(2):
        axis = axes[p][0]
        for d in (0, 1):
            s1[p, d] = block(p, d, (spot[axis] + 2) % 4)
            made[1, p, d] = copy(0, p, d, s1.at[p, d], r1.at[p, d], moved(spot, axis, 1 - 2 * d))
    for p in range(2):
        axis = axes[p][0]
        for d in (0, 1):
            near = (spot[axis] + 1 + 2 * d) % 4
            made[1, p, d].wait_recv()
            s2[p, d, d] = (block(p, d, near).astype(f32) + r1[p, d].astype(f32)).astype(bf)
            s2[p, d, 1 - d] = block(p, 1 - d, near)
            made[2, p, d] = copy(1, p, d, s2.at[p, d], r2.at[p, d], moved(spot, axis, 1 - 2 * d))
    for p in range(2):
        made[2, p, 0].wait_recv()
        made[2, p, 1].wait_recv()
        for m in (0, 1):
            acc[p, m] = (block(p, m, spot[axes[p][0]]).astype(f32)
                         + r2[p, 0, m].astype(f32) + r2[p, 1, m].astype(f32))
        axis = axes[p][1]
        for d in (0, 1):
            s3[p, d] = acc[p, d, :, (spot[axis] + 2) % 4].astype(bf)
            made[3, p, d] = copy(2, p, d, s3.at[p, d], r3.at[p, d], moved(spot, axis, 1 - 2 * d))
    for p in range(2):
        axis = axes[p][1]
        for d in (0, 1):
            near = (spot[axis] + 1 + 2 * d) % 4
            made[3, p, d].wait_recv()
            s4[p, d, d] = (acc[p, d, :, near] + r3[p, d].astype(f32)).astype(bf)
            s4[p, d, 1 - d] = acc[p, 1 - d, :, near].astype(bf)
            made[4, p, d] = copy(3, p, d, s4.at[p, d], r4.at[p, d], moved(spot, axis, 1 - 2 * d))
    for p in range(2):
        axis = axes[p][1]
        made[4, p, 0].wait_recv()
        made[4, p, 1].wait_recv()
        acc2[p] = acc[p, :, :, spot[axis]] + r4[p, 0].astype(f32) + r4[p, 1].astype(f32)
        s5[p] = acc2[p, :, 1 - xh].astype(bf)
        made[5, p, 0] = copy(4, p, 0, s5.at[p], r5.at[p], moved(spot, 0, 2))
    for p in range(2):
        made[5, p, 0].wait_recv()
        got[:, :, cols[p]] = acc2[p, :, xh] + r5[p].astype(f32)
    for each in made.values():
        each.wait_send()


def kv_scatter(terms, collective_id):
    bf, f32 = jnp.bfloat16, jnp.float32
    v = pltpu.VMEM
    return pl.pallas_call(
        kv_scatter_kernel,
        out_shape=jax.ShapeDtypeStruct((2, 64, 512), f32),
        in_specs=[pl.BlockSpec(memory_space=pltpu.VMEM)],
        out_specs=pl.BlockSpec(memory_space=pltpu.VMEM),
        scratch_shapes=[
            v((2, 2, 2, 4, 64, 256), bf), v((2, 2, 2, 4, 64, 256), bf),
            v((2, 2, 2, 2, 4, 64, 256), bf), v((2, 2, 2, 2, 4, 64, 256), bf),
            v((2, 2, 2, 64, 256), bf), v((2, 2, 2, 64, 256), bf),
            v((2, 2, 2, 2, 64, 256), bf), v((2, 2, 2, 2, 64, 256), bf),
            v((2, 2, 64, 256), bf), v((2, 2, 64, 256), bf),
            v((2, 2, 2, 4, 64, 256), f32), v((2, 2, 2, 64, 256), f32),
            pltpu.SemaphoreType.DMA((5, 2, 2)),
            pltpu.SemaphoreType.DMA((5, 2, 2)),
        ],
        compiler_params=pltpu.CompilerParams(
            collective_id=collective_id, has_side_effects=True, vmem_limit_bytes=48 * 1024 * 1024),
    )(terms)


BK = 512
ROWS = 512
HD = 64
KV = 4


def last(left, right):
    return lax.dot_general(left, right, (((1,), (1,)), ((), ())), preferred_element_type=jnp.float32)


def first(left, right):
    return lax.dot_general(left, right, (((0,), (0,)), ((), ())), preferred_element_type=jnp.float32)


def allowed_in(block, start, spot):
    columns = block * BK + lax.broadcasted_iota(jnp.int32, (ROWS, BK), 1)
    return (columns >= start) & (columns <= spot)


def forward_kernel(bounds, q, kv, marks, out, lse, top, total):
    micro = pl.program_id(0)
    start, spot = marks[0, :, 0:1], marks[0, :, 1:2]
    top[...] = jnp.full_like(top, -1e30)
    total[...] = jnp.zeros_like(total)
    out[...] = jnp.zeros_like(out)

    def step(block, carry):
        keep = allowed_in(block, start, spot)
        rows = pl.ds(pl.multiple_of(block * BK, BK), BK)
        for h in range(KV):
            s = last(q[0, h], kv[0, rows, h * HD : (h + 1) * HD]) * (HD**-0.5)
            s = jnp.where(keep, s, -1e30)
            high = jnp.maximum(top[h], jnp.max(s, axis=1, keepdims=True))
            fade = jnp.exp(top[h] - high)
            e = jnp.where(keep, jnp.exp(s - high), 0.0)
            total[h] = total[h] * fade + jnp.sum(e, axis=1, keepdims=True)
            out[0, h] = out[0, h] * fade + jnp.dot(
                e.astype(jnp.bfloat16), kv[0, rows, 256 + h * HD : 256 + (h + 1) * HD],
                preferred_element_type=jnp.float32)
            top[h] = high
        return carry

    lax.fori_loop(bounds[micro, 0], bounds[micro, 1], step, 0)
    for h in range(KV):
        out[0, h] = out[0, h] / total[h]
        lse[0, h] = top[h] + jnp.log(total[h])


def backward_kernel(bounds, q, kv, marks, out, lse, dout, dq, terms, lean):
    micro = pl.program_id(0)
    start, spot = marks[0, :, 0:1], marks[0, :, 1:2]
    dq[...] = jnp.zeros_like(dq)
    terms[...] = jnp.zeros_like(terms)
    for h in range(KV):
        lean[h] = jnp.sum(out[0, h] * dout[0, h].astype(jnp.float32), axis=1, keepdims=True)

    def step(block, carry):
        keep = allowed_in(block, start, spot)
        rows = pl.ds(pl.multiple_of(block * BK, BK), BK)
        keys, values = [], []
        for h in range(KV):
            k = kv[0, rows, h * HD : (h + 1) * HD]
            v = kv[0, rows, 256 + h * HD : 256 + (h + 1) * HD]
            s = last(q[0, h], k) * (HD**-0.5)
            p = jnp.where(keep, jnp.exp(jnp.where(keep, s - lse[0, h], -1e30)), 0.0)
            dp = last(dout[0, h], v)
            ds = (p * (dp - lean[h])).astype(jnp.bfloat16)
            dq[0, h] += jnp.dot(ds, k, preferred_element_type=jnp.float32) * (HD**-0.5)
            keys.append(first(ds, q[0, h]) * (HD**-0.5))
            values.append(first(p.astype(jnp.bfloat16), dout[0, h]))
        terms[0, rows, :] = jnp.concatenate(keys + values, axis=1).astype(jnp.bfloat16)
        return carry

    lax.fori_loop(bounds[micro, 0], bounds[micro, 1], step, 0)


def each(shape):
    zeros = (0,) * (len(shape) - 1)
    return pl.BlockSpec((1,) + shape[1:], lambda m, b: (m,) + zeros)


def attend(bounds, q, kv, marks):
    f32 = jnp.float32
    shapes = [(2, KV, ROWS, HD), (2, KV, ROWS, 1)]
    return pl.pallas_call(
        forward_kernel,
        out_shape=[jax.ShapeDtypeStruct(s, f32) for s in shapes],
        grid_spec=pltpu.PrefetchScalarGridSpec(
            num_scalar_prefetch=1, grid=(2,),
            in_specs=[each(q.shape), each(kv.shape), each(marks.shape)],
            out_specs=[each(s) for s in shapes],
            scratch_shapes=[pltpu.VMEM((KV, ROWS, 1), f32), pltpu.VMEM((KV, ROWS, 1), f32)],
        ),
        compiler_params=pltpu.CompilerParams(vmem_limit_bytes=48 * 1024 * 1024),
    )(bounds, q, kv, marks)


def attend_back(bounds, q, kv, marks, out, lse, dout):
    f32 = jnp.float32
    shapes = [((2, KV, ROWS, HD), f32), ((2, 2048, 512), jnp.bfloat16)]
    return pl.pallas_call(
        backward_kernel,
        out_shape=[jax.ShapeDtypeStruct(s, d) for s, d in shapes],
        grid_spec=pltpu.PrefetchScalarGridSpec(
            num_scalar_prefetch=1, grid=(2,),
            in_specs=[each(a.shape) for a in (q, kv, marks, out, lse, dout)],
            out_specs=[each(s) for s, _ in shapes],
            scratch_shapes=[pltpu.VMEM((KV, ROWS, 1), f32)],
        ),
        compiler_params=pltpu.CompilerParams(vmem_limit_bytes=48 * 1024 * 1024),
    )(bounds, q, kv, marks, out, lse, dout)


TB = 32
D = 2048
NORM_EPS = 1e-05


def stream(ref, s):
    return ref[:, s * D : (s + 1) * D].astype(jnp.float32)


def weight(mix, k, s, j):
    return mix[k * 24 + s * 6 + j]


def entry_of(parts, mix, k):
    return sum(weight(mix, k, s, 0) * parts[s] for s in range(4))


def normed_of(entry):
    center = entry - jnp.mean(entry, axis=-1, keepdims=True)
    inverse = lax.rsqrt(jnp.mean(center * center, axis=-1, keepdims=True) + NORM_EPS)
    return center * inverse, inverse


def norm_back(grad, normed, inverse):
    return inverse * (
        grad
        - jnp.mean(grad, axis=-1, keepdims=True)
        - normed * jnp.mean(grad * normed, axis=-1, keepdims=True)
    )


def mixed_out(parts, branch, mix, k, t):
    return sum(weight(mix, k, s, 2 + t) * parts[s] for s in range(4)) + weight(mix, k, t, 1) * branch


def inner(a, b):
    both = a * b
    folded = both[:, 0:128]
    for j in range(1, D // 128):
        folded = folded + both[:, j * 128 : (j + 1) * 128]
    return jnp.sum(folded, axis=0, keepdims=True)


def note(ref, row, value):
    ref[row : row + 1, :] += value


def start_notes(ref):
    @pl.when(pl.program_id(0) == 0)
    def _():
        ref[...] = jnp.zeros_like(ref)


def open_kernel(mix, tokens, entry):
    parts = [stream(tokens, s) for s in range(4)]
    entry[...] = normed_of(entry_of(parts, mix, 0))[0].astype(jnp.bfloat16)


def middle_kernel(mix, tokens, branch, middle, entry):
    parts = [stream(tokens, s) for s in range(4)]
    y = branch[...]
    x = None
    for t in range(4):
        out = mixed_out(parts, y, mix, 0, t)
        middle[:, t * D : (t + 1) * D] = out
        term = weight(mix, 1, t, 0) * out
        x = term if x is None else x + term
    entry[...] = normed_of(x)[0].astype(jnp.bfloat16)


def close_kernel(mix, middle, branch, coming, fresh, grad, notes):
    start_notes(notes)
    y = branch[...]
    e = None
    for t in range(4):
        g = stream(coming, t)
        fresh[:, t * D : (t + 1) * D] = mixed_out(
            [stream(middle, s) for s in range(4)], y, mix, 1, t).astype(jnp.bfloat16)
        term = weight(mix, 1, t, 1) * g
        e = term if e is None else e + term
        note(notes, t, inner(y, g))
        for s in range(4):
            note(notes, 4 + 4 * s + t, inner(stream(middle, s), g))
    grad[...] = e.astype(jnp.bfloat16)


def between_kernel(mix, tokens, middle, coming, dn, branch, middle_grad, grad, notes):
    start_notes(notes)
    parts = [stream(middle, s) for s in range(4)]
    normed, inverse = normed_of(entry_of(parts, mix, 1))
    dx = norm_back(dn[...], normed, inverse)
    y = branch[...]
    e = None
    for s in range(4):
        note(notes, s, inner(stream(middle, s), dx))
        g = sum(weight(mix, 1, s, 2 + t) * stream(coming, t) for t in range(4)) + weight(mix, 1, s, 0) * dx
        middle_grad[:, s * D : (s + 1) * D] = g
        term = weight(mix, 0, s, 1) * g
        e = term if e is None else e + term
        note(notes, 4 + s, inner(y, g))
        for r in range(4):
            note(notes, 8 + 4 * r + s, inner(stream(tokens, r), g))
    grad[...] = e.astype(jnp.bfloat16)


def last_kernel(mix, tokens, middle_grad, dn, tokens_grad, notes):
    start_notes(notes)
    parts = [stream(tokens, s) for s in range(4)]
    normed, inverse = normed_of(entry_of(parts, mix, 0))
    dx = norm_back(dn[...], normed, inverse)
    for s in range(4):
        note(notes, s, inner(stream(tokens, s), dx))
        tokens_grad[:, s * D : (s + 1) * D] = (
            sum(weight(mix, 0, s, 2 + t) * stream(middle_grad, t) for t in range(4)) + weight(mix, 0, s, 0) * dx)


def call(kernel, mix, arrays, outs, notes=0):
    rows = arrays[0].shape[0]
    shapes = [jax.ShapeDtypeStruct((rows, n), d) for n, d in outs]
    specs = [pl.BlockSpec((TB, n), lambda i: (i, 0)) for n, _ in outs]
    if notes:
        shapes.append(jax.ShapeDtypeStruct((notes, 128), jnp.float32))
        specs.append(pl.BlockSpec((notes, 128), lambda i: (0, 0)))
    return pl.pallas_call(
        kernel,
        out_shape=shapes,
        grid=(rows // TB,),
        in_specs=[pl.BlockSpec(memory_space=pltpu.SMEM)]
        + [pl.BlockSpec((TB, a.shape[1]), lambda i: (i, 0)) for a in arrays],
        out_specs=specs,
        compiler_params=pltpu.CompilerParams(vmem_limit_bytes=48 * 1024 * 1024),
    )(mix, *arrays)


def rotary(values, spots, sign):
    half = values.shape[-1] // 2
    freq = jnp.exp(
        jnp.arange(half, dtype=jnp.float32) * (-2.0 * math.log(THETA_BASE) / values.shape[-1])
    )
    angle = spots[:, None] * freq[None, :]
    cosine = jnp.cos(angle)[:, None, :]
    sine = sign * jnp.sin(angle)[:, None, :]
    first_half = values[..., :half]
    second_half = values[..., half:]
    return jnp.concatenate(
        [first_half * cosine - second_half * sine, second_half * cosine + first_half * sine], axis=-1
    )


def adam(weight, grad, first, second, factor, rate, decay):
    grad = grad * factor
    first = BETA_ONE * first + (1.0 - BETA_ONE) * grad
    second = BETA_TWO * second + (1.0 - BETA_TWO) * grad * grad
    ahead = first / (1.0 - BETA_ONE**STEP)
    scaled = second / (1.0 - BETA_TWO**STEP)
    weight = weight - rate * (ahead / (jnp.sqrt(scaled) + ADAM_EPS) + decay * weight)
    return (weight, first, second)


def padded(columns):
    shape = columns.shape[:-1]
    split = columns.reshape(shape + (128, 44))
    split = jnp.pad(split, ((0, 0),) * len(shape) + ((0, 0), (0, 4)))
    return split.reshape(shape + (128 * 48,))


def unpadded(columns):
    shape = columns.shape[:-1]
    return columns.reshape(shape + (128, 48))[..., :44].reshape(shape + (FF,))


def head_rows(flat):
    return flat.reshape(2, 64, KV, 8, HD).transpose(0, 2, 3, 1, 4).reshape(2, KV, ROWS, HD)


def head_flat(rows):
    return rows.reshape(2, KV, 8, 64, HD).transpose(0, 3, 1, 2, 4).reshape(128, 2048)


def left_side(tokens_by_rows, subs):
    turned = tokens_by_rows.T.reshape(2, 4, 4, 2, 2, subs, 16, 128)
    return turned.transpose(4, 5, 0, 3, 1, 2, 6, 7).reshape(2, subs, 4, 4, 4, 16, 128)


def body(streams, doc_start, cotangent, mixing, w_project, w_output, w_expand, w_reduce,
         first_mixing, second_mixing, first_project, second_project, first_output, second_output,
         first_expand, second_expand, first_reduce, second_reduce):
    bf, f32 = jnp.bfloat16, jnp.float32
    anchor = lax.axis_index("ctx") * 64
    tokens = streams.reshape(128, 8192)
    coming = cotangent.reshape(128, 8192)
    starts = doc_start.reshape(2, 64)
    places = anchor + jnp.arange(64, dtype=jnp.int32)
    spots = (places[None, :] - starts).astype(f32).reshape(128)
    mix = mixing.reshape(48)

    bf_expand = w_expand.astype(bf)
    shards = [
        w_project.astype(bf),
        w_output.astype(bf),
        jnp.concatenate([padded(bf_expand[:, :FF]), padded(bf_expand[:, FF:])], axis=1),
        jnp.pad(w_reduce.astype(bf), ((0, 4), (0, 0))),
    ]
    gathered = gather(shards, 1)
    project, output, expand = (g.reshape(2048, g.shape[-1]) for g in gathered[:3])
    reduce = gathered[3].reshape(6144, 2048)

    (entry_one,) = call(open_kernel, mix, [tokens], [(2048, bf)])
    joined = jnp.dot(entry_one, project, preferred_element_type=f32)
    query = head_rows(rotary(joined[:, :2048].reshape(128, H, HD), spots, 1.0).astype(bf).reshape(128, 2048))
    keys = rotary(joined[:, 2048:2304].reshape(128, KV, HD), spots, 1.0).astype(bf).reshape(128, 256)
    own = jnp.concatenate([keys, joined[:, 2304:].astype(bf)], axis=1).reshape(2, 64, 512)
    kv = kv_gather(own, 2).reshape(2, 2048, 512)
    bounds = jnp.stack([starts[:, 0] // BK, jnp.broadcast_to((anchor + 63) // BK + 1, (2,))], axis=1).astype(jnp.int32)
    marks = jnp.stack([jnp.tile(starts, (1, 8)), jnp.broadcast_to(jnp.tile(places, 8), (2, ROWS))], axis=2)
    mixed, lse = attend(bounds, query, kv, marks)
    attended = head_flat(mixed.astype(bf))
    branch_one = jnp.dot(attended, output, preferred_element_type=f32)
    middle, entry_two = call(middle_kernel, mix, [tokens, branch_one], [(8192, f32), (2048, bf)])
    opened = jnp.dot(entry_two, expand, preferred_element_type=f32)
    gate, upper = opened[:, :6144], opened[:, 6144:]
    sigma = jax.nn.sigmoid(gate)
    hidden = (gate * sigma * upper).astype(bf)
    branch_two = jnp.dot(hidden, reduce, preferred_element_type=f32)
    fresh, grad_two, notes_two = call(
        close_kernel, mix, [middle, branch_two, coming], [(8192, bf), (2048, bf)], 24)

    back_hidden = lax.dot_general(grad_two, reduce, (((1,), (1,)), ((), ())), preferred_element_type=f32)
    opened_grad = jnp.concatenate(
        [back_hidden * upper * sigma * (1.0 + gate * (1.0 - sigma)), back_hidden * gate * sigma], axis=1).astype(bf)
    dn_two = lax.dot_general(opened_grad, expand, (((1,), (1,)), ((), ())), preferred_element_type=f32)
    middle_grad, grad_one, notes_one = call(
        between_kernel, mix, [tokens, middle, coming, dn_two, branch_one], [(8192, f32), (2048, bf)], 24)
    attended_grad = lax.dot_general(
        grad_one, output, (((1,), (1,)), ((), ())), preferred_element_type=f32).astype(bf)
    query_grad, terms = attend_back(bounds, query, kv, marks, mixed, lse, head_rows(attended_grad))
    kv_grad = kv_scatter(terms.reshape(2, 2, 4, 4, 64, 512), 3).reshape(128, 512)
    joined_grad = jnp.concatenate(
        [
            rotary(head_flat(query_grad).reshape(128, H, HD), spots, -1.0).reshape(128, 2048),
            rotary(kv_grad[:, :256].reshape(128, KV, HD), spots, -1.0).reshape(128, 256),
            kv_grad[:, 256:],
        ], axis=1).astype(bf)
    dn_one = lax.dot_general(joined_grad, project, (((1,), (1,)), ((), ())), preferred_element_type=f32)
    tokens_grad, notes_zero = call(last_kernel, mix, [tokens, middle_grad, dn_one], [(8192, f32)], 8)

    zero, one, two = (jnp.sum(n, axis=1) for n in (notes_zero, notes_one, notes_two))
    mix_grad = jnp.stack([
        jnp.concatenate([zero[:4, None], one[4:8, None], one[8:24].reshape(4, 4)], axis=1),
        jnp.concatenate([one[:4, None], two[:4, None], two[4:20].reshape(4, 4)], axis=1),
    ])
    vector = jnp.pad(mix_grad.reshape(1, 48), ((0, 7), (0, 80)))
    lhs = jnp.concatenate(
        [left_side(hidden, 3), left_side(entry_two, 1), left_side(attended, 1), left_side(entry_one, 1)], axis=1)
    rhs = jnp.concatenate([grad_two, opened_grad, grad_one, joined_grad], axis=1)
    grads, total = scatter(lhs, rhs, vector, 4)

    def units(lo, hi):
        return grads[lo:hi].transpose(1, 0, 2).reshape(16, (hi - lo) * W)

    reduce_grad = grads[:12].reshape(3, 4, 16, W).transpose(0, 2, 1, 3).reshape(48, 2048)[:44]
    expand_grad = units(12, 36)
    expand_grad = jnp.concatenate([unpadded(expand_grad[:, :6144]), unpadded(expand_grad[:, 6144:])], axis=1)
    output_grad = units(36, 40)
    project_grad = units(40, 45)
    mix_total = total[0, :48].reshape(2, 4, 6)
    norm = jnp.sqrt(jnp.sum(total[7]) + jnp.sum(mix_total * mix_total))
    factor = THRESHOLD / jnp.maximum(norm, THRESHOLD)
    mix_new = adam(mixing, mix_total, first_mixing, second_mixing, factor, RATE_MIXING, 0.0)
    proj_new = adam(w_project, project_grad, first_project, second_project, factor, RATE_MATRIX, DECAY_MATRIX)
    outp_new = adam(w_output, output_grad, first_output, second_output, factor, RATE_MATRIX, DECAY_MATRIX)
    expd_new = adam(w_expand, expand_grad, first_expand, second_expand, factor, RATE_MATRIX, DECAY_MATRIX)
    redc_new = adam(w_reduce, reduce_grad, first_reduce, second_reduce, factor, RATE_MATRIX, DECAY_MATRIX)
    return (fresh.reshape(streams.shape), tokens_grad.reshape(streams.shape), norm,
            *mix_new, *proj_new, *outp_new, *expd_new, *redc_new)


def solution(mesh):
    acts = P(None, "fsdp", "ctx", None, None)
    rows = P(("ctx", "fsdp"), None)
    return jax.shard_map(
        body,
        mesh=mesh,
        in_specs=(acts, P(None, "fsdp", "ctx"), acts, P()) + (rows,) * 4 + (P(), P()) + (rows,) * 8,
        out_specs=(acts, acts, P(), P(), P(), P()) + (rows,) * 12,
        check_vma=False,
    )
```

time: 5580 us -> 811 us (0.15)
  waiting for transfers between devices: 3690 us -> 0 us
  blocking collectives: 958 us -> 0 us
  Pallas kernels: 0 us -> 575 us
  matrix products: 468 us -> 95.4 us
  other arithmetic: 158 us -> 38.2 us
  local copies, waits for them, and re-layouts: 181 us -> 85.3 us
  starting transfers between devices: 87.7 us -> 0 us
    all_gather x16 -> x0, waiting for transfers between devices: 2160 us -> none  [the longest x2 436 us: body(): lax.all_gather(held[2], ('ctx', 'fsdp'), axis=0, tiled=True)]
    reduce_scatter x3 -> x0, waiting for transfers between devices: 1280 us -> none  [the longest x1 916 us: body(): lax.psum_scatter(make_rows((stacked[0], stacked[1], stacked[2]), (stacked...]
    unnamed x1 -> x0, blocking collectives: 883 us -> none
    pallas_call x0 -> x11, Pallas kernels: none -> 575 us  [the longest x1 214 us: gather(): pl.pallas_call(functools.partial(gather_kernel, n), out_shape=[jax.ShapeD...]
    dot_general x60 -> x8, matrix products: 468 us -> 95.4 us  [the longest x1 24.1 us: body(): lax.dot_general(opened_grad, expand, (((1,), (1,)), ((), ())), preferred_...]
    unnamed x34 -> x0, waiting for transfers between devices: 248 us -> none
    unnamed x347 -> x89, local copies, waits for them, and re-layouts: 159 us -> 23.8 us
    unnamed x13 -> x0, starting transfers between devices: 86.7 us -> none
  transfers between devices with their start and end apart: 32 -> 0, of which waited for: 20 -> 0; matrix products, arithmetic and copies ran while one was open for 29% -> 0% of each run, Pallas kernels for 0% -> 0%
where the time goes in v1:
time: 811 us; the launch traced here: 799 us
  Pallas kernels  575 us (71%)
  matrix products  95.4 us (12%)
  local copies, waits for them, and re-layouts  85.3 us (11%)
  other arithmetic  38.2 us (5%)
    pallas_call x1, Pallas kernels, gather(): pl.pallas_call(functools.partial(gather_kernel, n), out_shape=[jax.ShapeD...  214 us
    pallas_call x1, Pallas kernels, scatter(): pl.pallas_call(scatter_kernel, out_shape=[jax.ShapeDtypeStruct((UNITS, 16...  195 us
    pallas_call x1, Pallas kernels, kv_scatter(): pl.pallas_call(kv_scatter_kernel, out_shape=jax.ShapeDtypeStruct((2, 64,...  72.8 us
    pallas_call x1, Pallas kernels, kv_gather(): pl.pallas_call(kv_gather_kernel, out_shape=jax.ShapeDtypeStruct((2, 2, 4,...  35.6 us
    pallas_call x5, Pallas kernels, call(): pl.pallas_call(kernel, out_shape=shapes, grid=(rows // TB,), in_specs=[pl...  30.3 us
    dot_general x1, matrix products, body(): lax.dot_general(opened_grad, expand, (((1,), (1,)), ((), ())), preferred_...  24.1 us
    unnamed x89, local copies, waits for them, and re-layouts  23.8 us
    dot_general x1, matrix products, body(): opened = jnp.dot(entry_two, expand, preferred_element_type=f32)  18.3 us

profile of v1, /device:TPU:0, one launch (start us, length us, event | category | flops | bytes accessed | tf_op | source)
XLA Modules:
  0.0 798.7 jit_solution(15348029890910888171)
XLA Ops:
  2.1 3.1 copy.149
  11.3 2.5 reshape.315
  24.4 214.4 %shard_map.314 = (bf16[2,4,4,2,2,16,2560]{6,5,4,3,2,1,0:T(8,128)(2,1)}, bf16[2,4,4,2,2,16,2048]{6,5,4,3,2,1,0:T(8,128)(2,1)}, bf16[2,4,4,2,2,16,12288]{6,5,4,3,2...) custom-call(bf16[16,2560]{1,0:T(8,128)(2,1)} %convert_element_type.46.refs_0_, ...), custom_call_target="tpu_custom_call" | custom-call | tf_op jit(solution)/shard_map/pallas_call | solution.py:163
  238.9 5.5 fusion.24
  248.3 35.6 %shard_map.315 = bf16[2,2,4,4,64,512]{5,4,3,2,1,0:T(8,128)(2,1)S(1)} custom-call(bf16[2,64,512]{2,1,0:T(8,128)(2,1)S(1)} %pad_maximum_fusion.4.shard), custom_call_target="tpu_custom_call" | custom-call | tf_op jit(solution)/shard_map/pallas_call | solution.py:538
  297.8 15.2 %shard_map.316 = (f32[2,4,512,64]{3,2,1,0:T(8,128)S(1)}, f32[2,4,512,1]{3,2,1,0:T(8,128)S(1)}) custom-call(s32[2,2]{1,0:T(2,128)S(1)} %stack.16.bounds, bf16[2,4,512,64]{3,2,1,0:T(8,128)(2,1)S(1)} %bitcast.120, bf16[2,2048,512]{2,1,0:T(8,128)(2,1)} %bitcast.116, s32[2,512,2]{2,1,0:T(8,128)S(1)} %pad_add_fusion.marks), custom_call_target="tpu_custom_call" | custom-call | tf_op jit(solution)/shard_map/pallas_call | solution.py:726
  316.6 2.7 reshape.325
  319.3 4.8 fusion.25.branch
  324.2 4.5 shard_map.317
  329.6 18.3 %fusion.26 = f32[128,12288]{1,0:T(8,128)S(1)} fusion(bf16[128,2048]{1,0:T(8,128)(2,1)S(1)} %get-tuple-element.42, bf16[2048,12288]{1,0:T(8,128)(2,1)} %bitcast.129), kind=kOutput, calls=%fused_computation.92 | convolution fusion | flops 6442450944 | bytes 57147392 | tf_op jit(solution)/shard_map/dot_general | solution.py:974
  348.0 12.7 %fusion.27.branch = f32[128,2048]{1,0:T(8,128)S(1)} fusion(bf16[6144,2048]{1,0:T(8,128)(2,1)} %bitcast.168, f32[128,12288]{1,0:T(8,128)S(1)} %fusion.26), kind=kOutput, calls=%fused_computation.93 | convolution fusion | flops 3225944064 | bytes 32505856 | tf_op jit(solution)/shard_map/dot_general | solution.py:978
  362.2 6.5 shard_map.318
  369.6 15.1 %constant_dynamic-update-slice_fusion.5 = (bf16[128,18944]{1,0:T(8,128)(2,1)}, bf16[128,6144]{1,0:T(8,128)(2,1)}, f32[128,6144]{1,0:T(8,128)}) fusion(bf16[128,18944]{1,0:T(8,128)(2,1)} %constant_dynamic-update-slice_fusion.6, f32[128,12288]{1,0:T(8,128)S(1)} %fusion.26, bf16[128,2048]{1,0:T(8,128)(2,1)S(1)} %get-tuple-element.46, ...), kind=kOutput, calls=%fused_computation.62 | convolution fusion | flops 3229089792 | bytes 38273024 | tf_op jit(solution)/shard_map/dot_general | solution.py:982
  384.7 4.5 constant_dynamic-update-slice_fusion.4
  389.3 24.1 %fusion.dn = f32[128,2048]{1,0:T(8,128)} fusion(bf16[2048,12288]{1,0:T(8,128)(2,1)} %bitcast.130, bf16[128,6144]{1,0:T(8,128)(2,1)} %get-tuple-element.148, bf16[128,6144]{1,0:T(8,128)(2,1)} %get-tuple-element.150), kind=kOutput, calls=%fused_computation | convolution fusion | flops 6448742400 | bytes 54525952 | tf_op jit(solution)/shard_map/dot_general | solution.py:985
  415.8 10.3 %shard_map.319 = (f32[128,8192]{1,0:T(8,128)}, bf16[128,2048]{1,0:T(8,128)(2,1)S(1)}, f32[24,128]{1,0:T(8,128)S(1)}) custom-call(f32[48]{0:T(128)S(1)} %reshape.311.mix, bf16[128,8192]{1,0:T(8,128)(2,1)S(1)} %bitcast.114, f32[128,8192]{1,0:T(8,128)} %get-tuple-element.41.middle, bf16[128,8192]{1,0:T(8,128)(2,1)} %bitcast.119, f32[128,2048]{1,0:T(8,128)S(1)} %copy-done.9, ...), custom_call_target="tpu_custom_call" | custom-call | tf_op jit(solution)/shard_map/pallas_call | solution.py:878
  426.8 7.1 convolution_convert_fusion
  433.9 2.8 reshape.331
  439.4 12.4 %shard_map.320 = (f32[2,4,512,64]{3,2,1,0:T(8,128)S(1)}, bf16[2,2048,512]{2,1,0:T(8,128)(2,1)}) custom-call(s32[2,2]{1,0:T(2,128)S(1)} %stack.16.bounds, bf16[2,4,512,64]{3,2,1,0:T(8,128)(2,1)S(1)} %bitcast.121, bf16[2,2048,512]{2,1,0:T(8,128)(2,1)} %bitcast.117, s32[2,512,2]{2,1,0:T(8,128)S(1)} %copy-done.8, f32[2,4,512,64]{3,2,1,0:T(8,128)} %copy-done.4, ...), custom_call_target="tpu_custom_call" | custom-call | tf_op jit(solution)/shard_map/pallas_call | solution.py:742
  455.3 72.8 %shard_map.321 = f32[2,64,512]{2,1,0:T(8,128)S(1)} custom-call(bf16[2,2,4,4,64,512]{5,4,3,2,1,0:T(8,128)(2,1)S(1)} %bitcast.123), custom_call_target="tpu_custom_call" | custom-call | tf_op jit(solution)/shard_map/pallas_call | solution.py:622
  528.4 4.1 copy.122
  532.5 3.4 reshape_reshape.4
  544.3 7.7 fusion.5.dn
  552.0 7.3 shard_map.322
  561.2 4.8 fusion.42
  566.0 2.6 copy.125
  568.7 3.1 copy.126
  572.9 3.0 pad_maximum_fusion.lhs
  575.9 194.5 %shard_map.323 = (f32[45,16,512]{2,1,0:T(8,128)}, f32[8,128]{1,0:T(8,128)}) custom-call(bf16[2,6,4,4,4,16,128]{6,5,4,3,2,1,0:T(8,128)(2,1)} %pad_maximum_fusion.lhs, bf16[128,18944]{1,0:T(8,128)(2,1)} %get-tuple-element.145.rhs, f32[8,128]{1,0:T(8,128)} %pad.19.mix), custom_call_target="tpu_custom_call" | custom-call | tf_op jit(solution)/shard_map/pallas_call | solution.py:447
  780.1 3.1 multiply_subtract_fusion
  788.2 6.2 reshape.339
  794.4 2.7 reshape.330
  (192 shorter events, 76.6 us)
Async XLA Ops:
  2.1 4.9 copy-start.22
  7.1 231.8 %copy-start.5 = (bf16[128,2048]{1,0:T(8,128)(2,1)}, bf16[128,2048]{1,0:T(8,128)(2,1)S(1)}, u32[]{:S(2)}) copy-start(bf16[128,2048]{1,0:T(8,128)(2,1)S(1)} %shard_map.313) | copy-start | bytes 1572868
  7.1 13.5 %copy-start.25 = (f32[44,2048]{1,0:T(8,128)S(1)}, f32[44,2048]{1,0:T(8,128)}, u32[]{:S(2)}) copy-start(f32[44,2048]{1,0:T(8,128)} %param.25) | copy-start | bytes 1081348
  238.9 7.3 copy-start.37
  248.3 37.6 %slice-start = ((f32[128,2560]{1,0:T(8,128)}), f32[128,2048]{1,0:T(8,128)S(1)}, s32[]{:S(2)}) async-start(f32[128,2560]{1,0:T(8,128)} %copy-done.21), calls=%async_computation | async-start | bytes 2097152 | tf_op jit(solution)/shard_map/slice | solution.py:964
  283.9 2.0 copy-start
  297.8 16.8 %copy-start.7 = (s32[2,512,2]{2,1,0:T(8,128)}, s32[2,512,2]{2,1,0:T(8,128)S(1)}, u32[]{:S(2)}) copy-start(s32[2,512,2]{2,1,0:T(8,128)S(1)} %pad_add_fusion.marks) | copy-start | bytes 24580
  313.0 2.0 copy-start.18
  329.6 18.4 %copy-start.11 = (bf16[128,2048]{1,0:T(8,128)(2,1)}, bf16[128,2048]{1,0:T(8,128)(2,1)S(1)}, u32[]{:S(2)}) copy-start(bf16[128,2048]{1,0:T(8,128)(2,1)S(1)} %get-tuple-element.42) | copy-start | bytes 1572868
  348.0 36.8 %copy-start.19 = (f32[128,12288]{1,0:T(8,128)}, f32[128,12288]{1,0:T(8,128)S(1)}, u32[]{:S(2)}) copy-start(f32[128,12288]{1,0:T(8,128)S(1)} %fusion.26) | copy-start | bytes 18874372
  348.0 12.8 %copy-start.24 = (bf16[2,1,64,4,2048]{4,3,2,1,0:T(4,128)(2,1)S(1)}, bf16[2,1,64,4,2048]{4,3,2,1,0:T(4,128)(2,1)}, u32[]{:S(2)}) copy-start(bf16[2,1,64,4,2048]{4,3,2,1,0:T(4,128)(2,1)} %param.20) | copy-start | bytes 6291460
  362.2 6.5 copy-start.1
  368.7 16.1 %copy-start.15 = (bf16[128,8192]{1,0:T(8,128)(2,1)}, bf16[128,8192]{1,0:T(8,128)(2,1)S(1)}, u32[]{:S(2)}) copy-start(bf16[128,8192]{1,0:T(8,128)(2,1)S(1)} %get-tuple-element.45) | copy-start | bytes 6291460
  453.1 2.2 copy-start.10
  532.5 7.6 copy-start.14
  566.0 5.8 copy-start.12
  568.7 3.5 copy-start.20
  568.7 3.8 copy-start.6
  575.9 199.9 %copy-start.26 = (f32[44,2048]{1,0:T(8,128)S(1)}, f32[44,2048]{1,0:T(8,128)}, u32[]{:S(2)}) copy-start(f32[44,2048]{1,0:T(8,128)} %param.25) | copy-start | bytes 1081348
  575.9 199.9 %copy-start.30 = (f32[44,2048]{1,0:T(8,128)S(1)}, f32[44,2048]{1,0:T(8,128)}, u32[]{:S(2)}) copy-start(f32[44,2048]{1,0:T(8,128)} %param.34) | copy-start | bytes 1081348
  575.9 199.9 %copy-start.31 = (f32[44,2048]{1,0:T(8,128)S(1)}, f32[44,2048]{1,0:T(8,128)}, u32[]{:S(2)}) copy-start(f32[44,2048]{1,0:T(8,128)} %param.35) | copy-start | bytes 1081348
  777.8 2.2 copy-start.23
  779.4 4.8 copy-start.29
  779.4 4.8 copy-start.34
  779.4 4.8 copy-start.35
  780.0 5.9 copy-start.28
  780.0 5.9 copy-start.32
  780.0 5.9 copy-start.33
  780.0 7.5 copy-start.36
  780.1 7.5 copy-start.38
  780.1 7.5 copy-start.39
  788.2 6.2 copy-start.16
  (9 other events, 10.8 us)
